TPU v7x, 256 devices: a whole 4x4x8 slice. The times are simulated.
256 devices in a mesh: row: 16 (over y, z_lo, core), col: 16 (over x, z_hi).
Axes of the slice: x: 4, y: 4, z: 8 (z_hi: 4, z_lo: 2; z = z_hi * 2 + z_lo), core: 2. Of those that a mesh axis runs over, the one named last changes fastest.
Arguments:
- query_single: bfloat16 [1024, 384], P('row'), may hold values from -6 to 6
- key_single: bfloat16 [4096, 384], P('col'), may hold values from -6 to 6
- query_weight: bfloat16 [384, 336], replicated, may hold values from -0.3125 to 0.3125
- key_weight: bfloat16 [384, 816], replicated, may hold values from -0.3125 to 0.3125
- pair_weight: bfloat16 [128, 12], replicated, may hold values from -1 to 1
- head_weight: float32 [12], replicated, may hold values from 0.2 to 2
- chain_bias: float32 [12], replicated, may hold values from -2 to 2
- pair: bfloat16 [1024, 4096, 128], P('row', 'col'), may hold values from -1000 to 1000
- residue_mask: int32 [4096], replicated, may hold values 0 or 1
- chain_index: int32 [4096], replicated, may hold values from 0 to 7, never falling along the last dimension, each value on 1 to 1024 neighbouring positions
- strip_offsets: int32 [16], replicated, may hold values from 0 to 4032, as said below
- grad_single_out: bfloat16 [1024, 192], P('row'), may hold values from -4 to 4
- grad_point_out: bfloat16 [1024, 288], P('row'), may hold values from -3 to 3
- grad_pair_out: bfloat16 [1024, 1536], P('row'), may hold values from -1 to 1
Outputs:
- grad_query_single: float32 [1024, 384], P('row')
- grad_key_single: float32 [4096, 384], P('col')
- grad_query_weight: float32 [384, 336], replicated
- grad_key_weight: float32 [384, 816], replicated
- grad_pair_weight: float32 [128, 12], replicated
- grad_pair: bfloat16 [1024, 4096, 128], P('row', 'col')
Inputs may be any that keep to these rules, and one draw needn't show every extreme that they name: `strip_offsets`: distinct multiples of 64; the first and the last strip of 64 residues are both among them.
All inputs are finite; a program needn't handle non-finite values.
Results may differ from a plain program's by a relative error of at most 0.012.
Values sent between devices are 32-bit elements; how exact they have to be, the bound alone decides.
No kernel may reach another device: no remote copies, remote signals or barrier semaphores. Data moves between devices by JAX's collectives and lax.ppermute only.
A program may use at most 64 MiB of HBM per device.

v0:
```python
import math
import jax
import jax.numpy as jnp
from jax import lax
from jax.sharding import PartitionSpec as P

H = 12
C = 16
P_SIZE = 4
PV = 8
DZ = 128
LOGIT_WEIGHT = math.sqrt(1.0 / 3.0)
MASKED_LOGIT = -100000.0


def local(
    query_single,
    key_single,
    query_weight,
    key_weight,
    pair_weight,
    head_weight,
    chain_bias,
    pair,
    residue_mask,
    chain_index,
    strip_offsets,
    grad_single_out,
    grad_point_out,
    grad_pair_out,
):
    query_rows = query_single.shape[0]
    key_rows = key_single.shape[0]
    head_cols = H * C
    point_cols = 3 * H * P_SIZE
    highest = lax.Precision.HIGHEST
    query_feats = jnp.dot(query_single, query_weight, preferred_element_type=jnp.float32).astype(
        jnp.bfloat16
    )
    key_feats = jnp.dot(key_single, key_weight, preferred_element_type=jnp.float32).astype(
        jnp.bfloat16
    )
    query_vec = query_feats[:, :head_cols].reshape(query_rows, H, C)
    query_pts = query_feats[:, head_cols:].reshape(query_rows, 3, H, P_SIZE)
    key_vec = key_feats[:, :head_cols].reshape(key_rows, H, C)
    value_vec = key_feats[:, head_cols : 2 * head_cols].reshape(key_rows, H, C)
    key_pts = key_feats[:, 2 * head_cols : 2 * head_cols + point_cols].reshape(
        key_rows, 3, H, P_SIZE
    )
    value_pts = key_feats[:, 2 * head_cols + point_cols :].reshape(key_rows, 3, H, PV)
    grad_vec = grad_single_out.reshape(query_rows, H, C)
    grad_pts = grad_point_out.reshape(query_rows, 3, H, PV)
    grad_pairs = grad_pair_out.reshape(query_rows, H, DZ)
    strip_begin = lax.dynamic_index_in_dim(strip_offsets, lax.axis_index("row"), 0, keepdims=False)
    key_begin = lax.axis_index("col") * key_rows
    query_live = lax.dynamic_slice_in_dim(residue_mask, strip_begin, query_rows, 0) == 1
    query_chain = lax.dynamic_slice_in_dim(chain_index, strip_begin, query_rows, 0)
    key_live = lax.dynamic_slice_in_dim(residue_mask, key_begin, key_rows, 0) == 1
    key_chain = lax.dynamic_slice_in_dim(chain_index, key_begin, key_rows, 0)
    live_pairs = query_live[:, None] & key_live[None, :]
    same_chain = (query_chain[:, None] == key_chain[None, :]).astype(jnp.float32)
    scalar = jnp.einsum("ihc,jhc->hij", query_vec, key_vec, preferred_element_type=jnp.float32)
    cross_term = jnp.einsum(
        "ixhp,jxhp->hij", query_pts, key_pts, preferred_element_type=jnp.float32
    )
    query_float = query_pts.astype(jnp.float32)
    key_float = key_pts.astype(jnp.float32)
    query_norm = jnp.sum(query_float * query_float, axis=(1, 3)).T
    key_norm = jnp.sum(key_float * key_float, axis=(1, 3)).T
    distance = query_norm[:, :, None] + key_norm[:, None, :] - 2.0 * cross_term
    pair_bias = jnp.einsum("ijc,ch->hij", pair, pair_weight, preferred_element_type=jnp.float32)
    point_coef = head_weight * (math.sqrt(2.0 / (9.0 * P_SIZE)) / 2.0)
    logits = LOGIT_WEIGHT * (
        scalar * C ** (-0.5) + pair_bias - point_coef[:, None, None] * distance
    )
    logits = logits + chain_bias[:, None, None] * same_chain[None]
    logits = jnp.where(live_pairs[None], logits, MASKED_LOGIT)
    row_top = lax.pmax(jnp.max(logits, axis=2), "col")
    upstream = jnp.einsum("ihc,jhc->hij", grad_vec, value_vec, preferred_element_type=jnp.float32)
    upstream = upstream + jnp.einsum(
        "ixhv,jxhv->hij", grad_pts, value_pts, preferred_element_type=jnp.float32
    )
    upstream = upstream + jnp.einsum(
        "ihc,ijc->hij", grad_pairs, pair, preferred_element_type=jnp.float32
    )
    exp_terms = jnp.exp(logits - row_top[:, :, None])
    row_total, moment = lax.psum(
        (jnp.sum(exp_terms, axis=2), jnp.sum(exp_terms * upstream, axis=2)), "col"
    )
    weights = exp_terms / row_total[:, :, None]
    centre = moment / row_total
    score_grad = jnp.where(live_pairs[None], weights * (upstream - centre[:, :, None]), 0.0)
    weight_bf = weights.astype(jnp.bfloat16)
    score_bf = score_grad.astype(jnp.bfloat16)
    scale_qk = LOGIT_WEIGHT * C ** (-0.5)
    grad_coef = -2.0 * LOGIT_WEIGHT * point_coef
    row_score = jnp.sum(score_bf, axis=2, dtype=jnp.float32)
    col_score = jnp.sum(score_bf, axis=1, dtype=jnp.float32)
    grad_qvec = scale_qk * jnp.einsum(
        "hij,jhc->ihc", score_bf, key_vec, preferred_element_type=jnp.float32
    )
    grad_qpts = grad_coef[None, None, :, None] * (
        query_float * row_score.T[:, None, :, None]
        - jnp.einsum("hij,jxhp->ixhp", score_bf, key_pts, preferred_element_type=jnp.float32)
    )
    query_part = jnp.concatenate(
        [grad_qvec.reshape(query_rows, -1), grad_qpts.reshape(query_rows, -1)], axis=1
    )
    query_grad = lax.psum(query_part, "col")
    grad_kvec = scale_qk * jnp.einsum(
        "hij,ihc->jhc", score_bf, query_vec, preferred_element_type=jnp.float32
    )
    grad_vvec = jnp.einsum("hij,ihc->jhc", weight_bf, grad_vec, preferred_element_type=jnp.float32)
    grad_kpts = grad_coef[None, None, :, None] * (
        key_float * col_score.T[:, None, :, None]
        - jnp.einsum("hij,ixhp->jxhp", score_bf, query_pts, preferred_element_type=jnp.float32)
    )
    grad_vpts = jnp.einsum(
        "hij,ixhv->jxhv", weight_bf, grad_pts, preferred_element_type=jnp.float32
    )
    key_part = jnp.concatenate(
        [
            grad_kvec.reshape(key_rows, -1),
            grad_vvec.reshape(key_rows, -1),
            grad_kpts.reshape(key_rows, -1),
            grad_vpts.reshape(key_rows, -1),
        ],
        axis=1,
    )
    bias_part = LOGIT_WEIGHT * jnp.einsum(
        "ijc,hij->ch", pair, score_bf, preferred_element_type=jnp.float32
    )
    key_weight_float = key_weight.astype(jnp.float32)
    key_single_float = key_single.astype(jnp.float32)
    key_grad = lax.psum(key_part, "row")
    grad_key_single = jnp.dot(key_grad, key_weight_float.T, precision=highest)
    grad_key_weight = lax.psum(jnp.dot(key_single_float.T, key_grad, precision=highest), "col")
    grad_pair_weight = lax.psum(bias_part, ("row", "col"))
    grad_query_single = jnp.dot(query_grad, query_weight.astype(jnp.float32).T, precision=highest)
    grad_query_weight = lax.psum(
        jnp.dot(query_single.astype(jnp.float32).T, query_grad, precision=highest), "row"
    )
    pair_grad = LOGIT_WEIGHT * jnp.einsum(
        "hij,ch->ijc", score_bf, pair_weight, preferred_element_type=jnp.float32
    )
    pair_grad = pair_grad + jnp.einsum(
        "hij,ihc->ijc", weight_bf, grad_pairs, preferred_element_type=jnp.float32
    )
    grad_pair = pair_grad.astype(jnp.bfloat16)
    return (
        grad_query_single,
        grad_key_single,
        grad_query_weight,
        grad_key_weight,
        grad_pair_weight,
        grad_pair,
    )


def solution(mesh):
    in_specs = (
        P("row", None),
        P("col", None),
        P(),
        P(),
        P(),
        P(),
        P(),
        P("row", "col", None),
        P(),
        P(),
        P(),
        P("row", None),
        P("row", None),
        P("row", None),
    )
    out_specs = (P("row", None), P("col", None), P(), P(), P(), P("row", "col", None))
    return jax.shard_map(local, mesh=mesh, in_specs=in_specs, out_specs=out_specs, check_vma=False)
```

profile of v0, /device:TPU:1, one launch (start us, length us, event | category | flops | bytes accessed | tf_op | source)
XLA Modules:
  0.0 589.7 jit_solution(5173191952428739225)
XLA Ops:
  7.2 1.3 dynamic_slice.16
  13.5 1.3 convolution_convert_fusion
  15.6 1.2 convolution_convert_fusion.1
  17.3 1.2 broadcast_multiply_fusion
  18.5 3.4 fusion.32
  23.4 41.9 %pmax.7 = f32[12,64]{1,0:T(8,128)S(1)} all-reduce(f32[12,64]{1,0:T(8,128)S(1)} %get-tuple-element.20), channel_id=1, replica_groups=mesh['row'=16,'col'=16] {'col'}, use_global_device_ids=true, to_apply=%region_3.4 | all-reduce | flops 768 | bytes 6144 | tf_op jit(solution)/shard_map/pmax | solution.py:78
  65.6 3.4 fusion.36
  70.0 2.5 fusion.17
  72.5 62.8 %all-reduce = (f32[12,64]{1,0:T(8,128)S(1)}, f32[12,64]{1,0:T(8,128)S(1)}) all-reduce(f32[12,64]{1,0:T(8,128)} %get-tuple-element.7, f32[12,64]{1,0:T(8,128)} %get-tuple-element.6), channel_id=1, replica_groups=mesh['row'=16,'col'=16] {'col'}, use_global_device_ids=true, to_apply=%region_7.8 | all-reduce | flops 1536 | bytes 12288 | tf_op jit(solution)/shard_map/psum | solution.py:87
  135.3 1.9 convert_reduce_fusion
  137.2 1.1 convolution_bitcast_fusion.4
  140.3 1.1 fusion.11
  143.7 134.9 %all-reduce.6.cloned.1.call-done = f32[256,816]{0,1:T(8,128)} async-done(((f32[256,816]{0,1:T(8,128)}), f32[256,816]{0,1:T(8,128)}) %all-reduce.6.cloned.1.call-update) | async-done | bytes 835600 | tf_op jit(solution)/shard_map/psum | solution.py:135
  278.6 3.0 convolution_bitcast_fusion
  281.7 1.3 fusion.18
  283.1 4.0 add_convert_fusion
  287.1 161.8 %all-reduce.10.cloned.1.call-done = (f32[64,336]{0,1:T(8,128)}, f32[384,816]{0,1:T(8,128)}) async-done(((f32[64,336]{0,1:T(8,128)}, f32[384,816]{0,1:T(8,128)}), (f32[64,336]{0,1:T(8,128)}, f32[384,816]{0,1:T(8,128)})) %all-reduce.10.cloned.1.call-update) | async-done | bytes 1339408 | tf_op jit(solution)/shard_map/psum | solution.py:109
  448.9 2.1 convolution_bitcast_fusion.3
  451.1 3.1 fusion.15
  454.2 82.8 %psum.55 = f32[128,12]{0,1:T(8,128)} all-reduce(f32[128,12]{0,1:T(8,128)S(1)} %fusion.15), channel_id=1, replica_groups=mesh['row'=16,'col'=16] {'row','col'}, use_global_device_ids=true, to_apply=%region_14.15 | all-reduce | flops 1536 | bytes 12288 | tf_op jit(solution)/shard_map/psum | solution.py:138
  537.0 1.8 fusion.38
  539.8 40.5 %all-reduce.8.cloned.1.call-done = f32[384,336]{0,1:T(8,128)} async-done(((f32[384,336]{0,1:T(8,128)}), f32[384,336]{0,1:T(8,128)}) %all-reduce.8.cloned.1.call-update) | async-done | bytes 516112 | tf_op jit(solution)/shard_map/psum | solution.py:140
  580.3 1.9 copy.89
  582.2 1.0 copy.90
  (84 shorter events, 12.3 us)
Async XLA Ops:
  7.2 6.4 %copy-start = (bf16[384,816]{0,1:T(8,128)(2,1)S(1)}, bf16[384,816]{0,1:T(8,128)(2,1)}, u32[]{:S(2)}) copy-start(bf16[384,816]{0,1:T(8,128)(2,1)} %param.17) | copy-start | bytes 1880068
  7.2 271.4 %all-reduce.6.cloned.1.call-start = ((), (), s32[]{:S(2)}) async-start(), calls=%async_computation | async-start | bytes 1671168 | tf_op jit(solution)/shard_map/psum | solution.py:135
  14.9 7.7 %copy-start.2 = (bf16[256,816]{0,1:T(8,128)(2,1)}, bf16[256,816]{0,1:T(8,128)(2,1)S(1)}, u32[]{:S(2)}) copy-start(bf16[256,816]{0,1:T(8,128)(2,1)S(1)} %convolution_convert_fusion) | copy-start | bytes 1253380
  15.6 7.1 %copy-start.5 = (bf16[256,192]{0,1:T(8,128)(2,1)}, bf16[256,192]{0,1:T(8,128)(2,1)S(1)}, u32[]{:S(2)}) copy-start(bf16[256,192]{0,1:T(8,128)(2,1)S(1)} %get-tuple-element.16) | copy-start | bytes 294916
  15.6 7.1 %copy-start.21 = (f32[12]{0:T(128)S(1)}, f32[12]{0:T(128)}, u32[]{:S(2)}) copy-start(f32[12]{0:T(128)} %param.20) | copy-start | bytes 148
  17.0 6.3 %copy-start.12 = (bf16[64,192]{0,1:T(8,128)(2,1)}, bf16[64,192]{0,1:T(8,128)(2,1)S(1)}, u32[]{:S(2)}) copy-start(bf16[64,192]{0,1:T(8,128)(2,1)S(1)} %copy.40) | copy-start | bytes 73732
  17.1 6.3 %copy-start.9 = (bf16[256,3,12,4]{0,3,2,1:T(4,128)(2,1)}, bf16[256,3,12,4]{0,3,2,1:T(4,128)(2,1)S(1)}, u32[]{:S(2)}) copy-start(bf16[256,3,12,4]{0,3,2,1:T(4,128)(2,1)S(1)} %reshape.125) | copy-start | bytes 221188
  18.5 46.8 %copy-start.16 = (bf16[64,288]{1,0:T(8,128)(2,1)S(1)}, bf16[64,288]{1,0:T(8,128)(2,1)}, u32[]{:S(2)}) copy-start(bf16[64,288]{1,0:T(8,128)(2,1)} %param.26) | copy-start | bytes 110596
  18.5 46.9 %copy-start.13 = (bf16[64,1536]{1,0:T(8,128)(2,1)S(1)}, bf16[64,1536]{1,0:T(8,128)(2,1)}, u32[]{:S(2)}) copy-start(bf16[64,1536]{1,0:T(8,128)(2,1)} %param.27) | copy-start | bytes 589828
  22.7 42.7 %copy-start.15 = (pred[64,256]{1,0:T(8,128)(4,1)}, pred[64,256]{1,0:T(8,128)(4,1)S(1)}, u32[]{:S(2)}) copy-start(pred[64,256]{1,0:T(8,128)(4,1)S(1)} %get-tuple-element.24) | copy-start | bytes 49156
  22.7 46.2 %copy-start.17 = (bf16[64,192]{1,0:T(8,128)(2,1)S(1)}, bf16[64,192]{1,0:T(8,128)(2,1)}, u32[]{:S(2)}) copy-start(bf16[64,192]{1,0:T(8,128)(2,1)} %param.25) | copy-start | bytes 73732
  22.7 47.0 %slice-start = ((bf16[256,816]{0,1:T(8,128)(2,1)}), bf16[256,288]{0,1:T(8,128)(2,1)S(1)}, s32[]{:S(2)}) async-start(bf16[256,816]{0,1:T(8,128)(2,1)} %copy-done.2), calls=%async_computation.3 | async-start | bytes 294912 | tf_op jit(solution)/shard_map/slice | solution.py:50
  137.2 5.3 copy-start.19
  137.2 5.3 copy-start.20
  137.2 5.6 copy-start.6
  137.2 141.4 %copy-start.7 = (bf16[256,384]{1,0:T(8,128)(2,1)S(1)}, bf16[256,384]{1,0:T(8,128)(2,1)}, u32[]{:S(2)}) copy-start(bf16[256,384]{1,0:T(8,128)(2,1)} %param.15) | copy-start | bytes 589828
  141.4 140.3 %copy-start.18 = (bf16[128,12]{0,1:T(8,128)(2,1)S(1)}, bf16[128,12]{0,1:T(8,128)(2,1)}, u32[]{:S(2)}) copy-start(bf16[128,12]{0,1:T(8,128)(2,1)} %param.18) | copy-start | bytes 9220
  142.4 306.5 %all-reduce.10.cloned.1.call-start = ((), (), s32[]{:S(2)}) async-start(), calls=%async_computation.2 | async-start | bytes 2850816 | tf_op jit(solution)/shard_map/psum | solution.py:109
  281.7 298.6 %all-reduce.8.cloned.1.call-start = ((), (), s32[]{:S(2)}) async-start(), calls=%async_computation.1 | async-start | bytes 1032192 | tf_op jit(solution)/shard_map/psum | solution.py:140
  283.0 165.9 %copy-start.14 = (bf16[64,384]{1,0:T(8,128)(2,1)S(1)}, bf16[64,384]{1,0:T(8,128)(2,1)}, u32[]{:S(2)}) copy-start(bf16[64,384]{1,0:T(8,128)(2,1)} %param.14) | copy-start | bytes 147460
  287.1 249.9 %copy-start.1 = (f32[256,816]{0,1:T(8,128)S(1)}, f32[256,816]{0,1:T(8,128)}, u32[]{:S(2)}) copy-start(f32[256,816]{0,1:T(8,128)} %all-reduce.6.cloned.1.call-done) | copy-start | bytes 2506756
  287.1 251.7 %copy-start.4 = (bf16[384,336]{0,1:T(8,128)(2,1)S(1)}, bf16[384,336]{0,1:T(8,128)(2,1)}, u32[]{:S(2)}) copy-start(bf16[384,336]{0,1:T(8,128)(2,1)} %param.16) | copy-start | bytes 774148
  448.9 89.9 %copy-start.8 = (f32[64,336]{0,1:T(8,128)S(1)}, f32[64,336]{0,1:T(8,128)}, u32[]{:S(2)}) copy-start(f32[64,336]{0,1:T(8,128)} %get-tuple-element.12) | copy-start | bytes 258052
  451.1 131.1 %copy-start.3 = (f32[384,816]{0,1:T(8,128)S(1)}, f32[384,816]{0,1:T(8,128)}, u32[]{:S(2)}) copy-start(f32[384,816]{0,1:T(8,128)} %get-tuple-element.28) | copy-start | bytes 3760132
  (2 other events, 9.9 us)
Sparse Core Ops, SparseCore 0:
  142.6 136.0 all-reduce.5
  282.1 166.7 all-reduce.9
  452.3 127.9 all-reduce.7
where the time goes:
time: 591 us; the launch traced here: 590 us
  waiting for transfers between devices  337 us (57%)
  blocking collectives  188 us (32%)
  matrix products  34.3 us (6%)
  between operations  16.1 us (3%)
  local copies, waits for them, and re-layouts  7.97 us (1%)
  other arithmetic  6.44 us (1%)
    psum x1, waiting for transfers between devices, local(): query_grad = lax.psum(query_part, 'col')  162 us
    psum x1, waiting for transfers between devices, local(): key_grad = lax.psum(key_part, 'row')  135 us
    psum x1, blocking collectives, local(): grad_pair_weight = lax.psum(bias_part, ('row', 'col'))  82.8 us
    psum x1, blocking collectives, local(): lax.psum((jnp.sum(exp_terms, axis=2), jnp.sum(exp_terms * upstream, axis=...  62.8 us
    pmax x1, blocking collectives, local(): row_top = lax.pmax(jnp.max(logits, axis=2), 'col')  41.9 us
    psum x1, waiting for transfers between devices, local(): lax.psum(jnp.dot(query_single.astype(jnp.float32).T, query_grad, precisio...  40.5 us
  transfers between devices with their start and end apart: 3, of which 3 were waited for; matrix products, arithmetic and copies ran while one was open for 2% of the time, Pallas kernels for 0%

commit v1 on v0

--- a/solution.py
+++ b/solution.py
@@ -132,7 +132,7 @@
     )
     key_weight_float = key_weight.astype(jnp.float32)
     key_single_float = key_single.astype(jnp.float32)
-    key_grad = lax.psum(key_part, "row")
+    key_grad = jnp.sum(lax.all_gather(key_part, "row"), axis=0)
     grad_key_single = jnp.dot(key_grad, key_weight_float.T, precision=highest)
     grad_key_weight = lax.psum(jnp.dot(key_single_float.T, key_grad, precision=highest), "col")
     grad_pair_weight = lax.psum(bias_part, ("row", "col"))

time: 591 us -> 567 us (0.959)
  waiting for transfers between devices: 337 us -> 292 us
  local copies, waits for them, and re-layouts: 7.97 us -> 23.6 us
  other arithmetic: 6.44 us -> 13.5 us
    psum x1 -> x0, waiting for transfers between devices: 135 us -> none  [local(): key_grad = lax.psum(key_part, 'row')]
    all_gather x0 -> x1, waiting for transfers between devices: none -> 92.6 us  [local(): key_grad = jnp.sum(lax.all_gather(key_part, 'row'), axis=0)]
    unnamed x48 -> x43, local copies, waits for them, and re-layouts: 3.85 us -> 20.1 us
    reduce_sum x0 -> x1, other arithmetic: none -> 7.26 us  [local(): key_grad = jnp.sum(lax.all_gather(key_part, 'row'), axis=0)]
where the time goes in v1:
time: 567 us; the launch traced here: 566 us
  waiting for transfers between devices  292 us (51%)
  blocking collectives  188 us (33%)
  matrix products  32.3 us (6%)
  local copies, waits for them, and re-layouts  23.6 us (4%)
  between operations  16.1 us (3%)
  other arithmetic  13.5 us (2%)
    psum x1, waiting for transfers between devices, local(): query_grad = lax.psum(query_part, 'col')  160 us
    all_gather x1, waiting for transfers between devices, local(): key_grad = jnp.sum(lax.all_gather(key_part, 'row'), axis=0)  92.6 us
    psum x1, blocking collectives, local(): grad_pair_weight = lax.psum(bias_part, ('row', 'col'))  82.8 us
    psum x1, blocking collectives, local(): lax.psum((jnp.sum(exp_terms, axis=2), jnp.sum(exp_terms * upstream, axis=...  62.9 us
    pmax x1, blocking collectives, local(): row_top = lax.pmax(jnp.max(logits, axis=2), 'col')  42 us
    psum x1, waiting for transfers between devices, local(): lax.psum(jnp.dot(query_single.astype(jnp.float32).T, query_grad, precisio...  39.5 us
    unnamed x43, local copies, waits for them, and re-layouts  20.1 us
  transfers between devices with their start and end apart: 3, of which 3 were waited for; matrix products, arithmetic and copies ran while one was open for 2% of the time, Pallas kernels for 0%

profile of v1, /device:TPU:1, one launch (start us, length us, event | category | flops | bytes accessed | tf_op | source)
XLA Modules:
  0.0 565.9 jit_solution(8547526131472682496)
XLA Ops:
  7.2 1.3 dynamic_slice.16
  13.6 1.2 convolution_convert_fusion.1
  14.8 1.3 convolution_convert_fusion
  16.7 1.2 broadcast_multiply_fusion
  17.8 3.4 fusion.31
  22.7 42.0 %pmax.7 = f32[12,64]{1,0:T(8,128)S(1)} all-reduce(f32[12,64]{1,0:T(8,128)S(1)} %get-tuple-element.20), channel_id=1, replica_groups=mesh['row'=16,'col'=16] {'col'}, use_global_device_ids=true, to_apply=%region_3.4 | all-reduce | flops 768 | bytes 6144 | tf_op jit(solution)/shard_map/pmax | solution.py:78
  64.9 3.4 fusion.35
  69.6 1.7 fusion.17
  71.4 62.9 %all-reduce = (f32[12,64]{1,0:T(8,128)S(1)}, f32[12,64]{1,0:T(8,128)S(1)}) all-reduce(f32[12,64]{1,0:T(8,128)S(1)} %get-tuple-element.7, f32[12,64]{1,0:T(8,128)S(1)} %get-tuple-element.6), channel_id=1, replica_groups=mesh['row'=16,'col'=16] {'col'}, use_global_device_ids=true, to_apply=%region_7.8 | all-reduce | flops 1536 | bytes 12288 | tf_op jit(solution)/shard_map/psum | solution.py:87
  134.4 1.7 convert_reduce_fusion
  141.7 92.6 %all-gather.3.cloned.1.call-done = f32[4096,816]{0,1:T(8,128)} async-done(((f32[256,816]{0,1:T(8,128)}), f32[4096,816]{0,1:T(8,128)}) %all-gather.3.cloned.1.call-update) | async-done | bytes 13369360 | tf_op jit(solution)/shard_map/all_gather | solution.py:135
  234.4 16.1 %copy.81 = f32[102,8,16,256]{3,2,1,0:T(8,128)} copy(f32[102,8,16,256]{3,1,2,0:T(8,128)} %bitcast.131) | data formatting | bytes 26738688
  250.5 7.3 %bitcast_reduce_fusion = f32[256,816]{0,1:T(8,128)S(1)} fusion(f32[102,8,16,256]{3,2,1,0:T(8,128)} %copy.81), kind=kLoop, calls=%fused_computation | loop fusion | flops 3133440 | bytes 14204928 | tf_op jit(solution)/shard_map/reduce_sum | solution.py:135
  257.7 1.9 convolution_bitcast_fusion
  259.9 1.3 fusion.18
  261.2 4.1 add_convert_fusion
  265.3 160.0 %all-reduce.7.cloned.1.call-done = (f32[64,336]{0,1:T(8,128)}, f32[384,816]{0,1:T(8,128)}) async-done(((f32[64,336]{0,1:T(8,128)}, f32[384,816]{0,1:T(8,128)}), (f32[64,336]{0,1:T(8,128)}, f32[384,816]{0,1:T(8,128)})) %all-reduce.7.cloned.1.call-update) | async-done | bytes 1339408 | tf_op jit(solution)/shard_map/psum | solution.py:109
  425.3 2.1 convolution_bitcast_fusion.3
  427.4 3.1 fusion.15
  430.5 82.8 %psum.47 = f32[128,12]{0,1:T(8,128)} all-reduce(f32[128,12]{0,1:T(8,128)S(1)} %fusion.15), channel_id=1, replica_groups=mesh['row'=16,'col'=16] {'row','col'}, use_global_device_ids=true, to_apply=%region_14.15 | all-reduce | flops 1536 | bytes 12288 | tf_op jit(solution)/shard_map/psum | solution.py:138
  513.3 1.8 fusion.37
  515.1 1.9 fusion.36
  517.0 39.5 %all-reduce.5.cloned.1.call-done = f32[384,336]{0,1:T(8,128)} async-done(((f32[384,336]{0,1:T(8,128)}), f32[384,336]{0,1:T(8,128)}) %all-reduce.5.cloned.1.call-update) | async-done | bytes 516112 | tf_op jit(solution)/shard_map/psum | solution.py:140
  556.5 1.9 copy.99
  (79 shorter events, 13.4 us)
Async XLA Ops:
  7.2 7.7 %copy-start = (bf16[384,816]{0,1:T(8,128)(2,1)S(1)}, bf16[384,816]{0,1:T(8,128)(2,1)}, u32[]{:S(2)}) copy-start(bf16[384,816]{0,1:T(8,128)(2,1)} %param.17) | copy-start | bytes 1880068
  7.2 227.2 %all-gather.3.cloned.1.call-start = ((), (), s32[]{:S(2)}) async-start(), calls=%async_computation.1 | async-start | bytes 14204928 | tf_op jit(solution)/shard_map/all_gather | solution.py:135
  16.2 6.5 %copy-start.1 = (bf16[256,816]{0,1:T(8,128)(2,1)}, bf16[256,816]{0,1:T(8,128)(2,1)S(1)}, u32[]{:S(2)}) copy-start(bf16[256,816]{0,1:T(8,128)(2,1)S(1)} %convolution_convert_fusion) | copy-start | bytes 1253380
  16.2 5.8 %copy-start.18 = (f32[12]{0:T(128)S(1)}, f32[12]{0:T(128)}, u32[]{:S(2)}) copy-start(f32[12]{0:T(128)} %param.20) | copy-start | bytes 148
  16.2 6.4 %copy-start.4 = (bf16[256,192]{0,1:T(8,128)(2,1)}, bf16[256,192]{0,1:T(8,128)(2,1)S(1)}, u32[]{:S(2)}) copy-start(bf16[256,192]{0,1:T(8,128)(2,1)S(1)} %get-tuple-element.16) | copy-start | bytes 294916
  16.4 6.3 %copy-start.10 = (bf16[64,192]{0,1:T(8,128)(2,1)}, bf16[64,192]{0,1:T(8,128)(2,1)S(1)}, u32[]{:S(2)}) copy-start(bf16[64,192]{0,1:T(8,128)(2,1)S(1)} %copy.61) | copy-start | bytes 73732
  16.5 6.2 %copy-start.7 = (bf16[256,3,12,4]{0,3,2,1:T(4,128)(2,1)}, bf16[256,3,12,4]{0,3,2,1:T(4,128)(2,1)S(1)}, u32[]{:S(2)}) copy-start(bf16[256,3,12,4]{0,3,2,1:T(4,128)(2,1)S(1)} %reshape.125) | copy-start | bytes 221188
  17.8 46.9 %copy-start.12 = (bf16[64,1536]{1,0:T(8,128)(2,1)S(1)}, bf16[64,1536]{1,0:T(8,128)(2,1)}, u32[]{:S(2)}) copy-start(bf16[64,1536]{1,0:T(8,128)(2,1)} %param.27) | copy-start | bytes 589828
  22.0 46.3 %copy-start.14 = (pred[64,256]{1,0:T(8,128)(4,1)}, pred[64,256]{1,0:T(8,128)(4,1)S(1)}, u32[]{:S(2)}) copy-start(pred[64,256]{1,0:T(8,128)(4,1)S(1)} %get-tuple-element.24) | copy-start | bytes 49156
  22.0 47.2 %copy-start.15 = (bf16[64,192]{1,0:T(8,128)(2,1)S(1)}, bf16[64,192]{1,0:T(8,128)(2,1)}, u32[]{:S(2)}) copy-start(bf16[64,192]{1,0:T(8,128)(2,1)} %param.25) | copy-start | bytes 73732
  22.7 46.6 %slice-start = ((bf16[256,816]{0,1:T(8,128)(2,1)}), bf16[256,288]{0,1:T(8,128)(2,1)S(1)}, s32[]{:S(2)}) async-start(bf16[256,816]{0,1:T(8,128)(2,1)} %copy-done.1), calls=%async_computation.3 | async-start | bytes 294912 | tf_op jit(solution)/shard_map/slice | solution.py:50
  69.2 65.1 %copy-start.9 = (bf16[64,288]{0,1:T(8,128)(2,1)}, bf16[64,288]{0,1:T(8,128)(2,1)S(1)}, u32[]{:S(2)}) copy-start(bf16[64,288]{0,1:T(8,128)(2,1)S(1)} %copy.66) | copy-start | bytes 110596
  69.3 65.0 %copy-start.11 = (bf16[64,192]{0,1:T(8,128)(2,1)}, bf16[64,192]{0,1:T(8,128)(2,1)S(1)}, u32[]{:S(2)}) copy-start(bf16[64,192]{0,1:T(8,128)(2,1)S(1)} %copy.65) | copy-start | bytes 73732
  71.4 67.7 %copy-start.8 = (bf16[256,3,12,4]{0,3,2,1:T(4,128)(2,1)S(1)}, bf16[256,3,12,4]{0,3,2,1:T(4,128)(2,1)}, u32[]{:S(2)}) copy-start(bf16[256,3,12,4]{0,3,2,1:T(4,128)(2,1)} %copy-done.7) | copy-start | bytes 221188
  71.4 67.7 %copy-start.17 = (f32[12]{0:T(128)S(1)}, f32[12]{0:T(128)}, u32[]{:S(2)}) copy-start(f32[12]{0:T(128)} %get-tuple-element.18) | copy-start | bytes 148
  134.3 6.5 %copy-start.5 = (bf16[256,192]{0,1:T(8,128)(2,1)S(1)}, bf16[256,192]{0,1:T(8,128)(2,1)}, u32[]{:S(2)}) copy-start(bf16[256,192]{0,1:T(8,128)(2,1)} %copy-done.4) | copy-start | bytes 294916
  140.4 284.9 %all-reduce.7.cloned.1.call-start = ((), (), s32[]{:S(2)}) async-start(), calls=%async_computation.2 | async-start | bytes 2850816 | tf_op jit(solution)/shard_map/psum | solution.py:109
  250.5 7.3 %copy-start.6 = (bf16[256,384]{1,0:T(8,128)(2,1)S(1)}, bf16[256,384]{1,0:T(8,128)(2,1)}, u32[]{:S(2)}) copy-start(bf16[256,384]{1,0:T(8,128)(2,1)} %param.15) | copy-start | bytes 589828
  250.5 9.4 %copy-start.16 = (bf16[128,12]{0,1:T(8,128)(2,1)S(1)}, bf16[128,12]{0,1:T(8,128)(2,1)}, u32[]{:S(2)}) copy-start(bf16[128,12]{0,1:T(8,128)(2,1)} %param.18) | copy-start | bytes 9220
  259.6 296.9 %all-reduce.5.cloned.1.call-start = ((), (), s32[]{:S(2)}) async-start(), calls=%async_computation | async-start | bytes 1032192 | tf_op jit(solution)/shard_map/psum | solution.py:140
  261.2 164.1 %copy-start.13 = (bf16[64,384]{1,0:T(8,128)(2,1)S(1)}, bf16[64,384]{1,0:T(8,128)(2,1)}, u32[]{:S(2)}) copy-start(bf16[64,384]{1,0:T(8,128)(2,1)} %param.14) | copy-start | bytes 147460
  265.3 249.8 %copy-start.3 = (bf16[384,336]{0,1:T(8,128)(2,1)S(1)}, bf16[384,336]{0,1:T(8,128)(2,1)}, u32[]{:S(2)}) copy-start(bf16[384,336]{0,1:T(8,128)(2,1)} %param.16) | copy-start | bytes 774148
  427.4 131.0 %copy-start.2 = (f32[384,816]{0,1:T(8,128)S(1)}, f32[384,816]{0,1:T(8,128)}, u32[]{:S(2)}) copy-start(f32[384,816]{0,1:T(8,128)} %get-tuple-element.28) | copy-start | bytes 3760132
Sparse Core Ops, SparseCore 0:
  140.5 93.8 all-gather.2
  259.7 165.4 all-reduce.6
  428.5 127.9 all-reduce.4
